TPU v7x, 32 devices: a whole 2x2x4 slice. The times are simulated.
32 devices in a mesh: groups: 2 (over y), chan: 4 (over z), win: 4 (over x, core).
Axes of the slice: x: 2, y: 2, z: 4, core: 2. Of those that a mesh axis runs over, the one named last changes fastest.
Arguments:
- tokens: bfloat16 [8, 1024, 512], P(('groups', 'win'), 'chan'), parts along dimension 0, may hold values from -6 to 6
- head_weight: bfloat16 [512, 1024], replicated, may hold values from -0.25 to 0.25
- target: bfloat16 [8, 512, 2048], P(('groups', 'win'), 'chan'), parts along dimension 0, may hold values from -6 to 6
- target_amp: bfloat16 [8, 512, 2048], P(('groups', 'win'), 'chan'), parts along dimension 0, may hold values from 0.29882812 to 3
- patch_ranks: int32 [8, 1024], P(('groups', 'win'), 'chan'), parts along dimension 0, may hold values from 0 to 1023, each once within a row
Outputs:
- grad_tokens: bfloat16 [8, 1024, 512], P(('groups', 'win'), 'chan'), parts along dimension 0
- grad_weight: float32 [1024, 1024], P(('groups', 'chan'), 'win'), parts along dimension 0
There are 2 independent parts, one for each index of `groups`. A program takes and returns all parts, laid end to end along the dimension named above; an argument that names none is the same for every part. Nothing has to cross between parts.
Inputs may be any that keep to these rules, and one draw needn't show every extreme that they name: `patch_ranks`: each window's row is a permutation of 0 to 1023; a patch is masked exactly when its rank is 256 or more.
All inputs are finite; a program needn't handle non-finite values.
Results may differ from a plain program's by a relative error of at most 0.0052.
Values sent between devices are 32-bit elements; how exact they have to be, the bound alone decides.
A program may use at most 128 MiB of HBM per device.

v0:
```python
from functools import partial
import math
import jax
import jax.numpy as jnp
from jax import lax
from jax.sharding import PartitionSpec as P

PATCH_C = 16
PATCH_S = 64
product = partial(jnp.einsum, precision=lax.Precision.HIGHEST)


def factor_pair(length):
    first = int(math.isqrt(length))
    while length % first:
        first -= 1
    return (first, length // first)


def section_one(length, direction):
    index = jnp.arange(length, dtype=jnp.int32)
    angles = (
        direction
        * 2.0
        * math.pi
        / length
        * (index[:, None] * index[None, :] % length).astype(jnp.float32)
    )
    cosine = jnp.cos(angles)
    sine = jnp.sin(angles)
    upper = jnp.stack([cosine, sine], axis=1)
    lower = jnp.stack([-sine, cosine], axis=1)
    return jnp.stack([upper, lower], axis=0)


def section_two(first, second, direction, scale):
    length = first * second
    outer = jnp.arange(first, dtype=jnp.int32)[:, None, None]
    inner = jnp.arange(second, dtype=jnp.int32)[None, :, None]
    final = jnp.arange(second, dtype=jnp.int32)[None, None, :]
    phase = (outer * inner + first * inner * final) % length
    angles = direction * 2.0 * math.pi / length * phase.astype(jnp.float32)
    cosine = jnp.cos(angles)
    sine = jnp.sin(angles)
    upper = jnp.stack([cosine, sine], axis=2)
    lower = jnp.stack([-sine, cosine], axis=2)
    return jnp.stack([upper, lower], axis=0) * scale


def time_forward(values):
    window_count, chan_rows, length = values.shape
    first, second = factor_pair(length)
    shaped = values.reshape(window_count, chan_rows, first, second)
    section = product("wcab,ask->wsckb", shaped, section_one(first, -1.0)[0])
    result = product("wsckb,skbtj->wtcjk", section, section_two(first, second, -1.0, 1.0))
    return result.reshape(window_count, 2, chan_rows, length)


def time_inverse(spectrum, scale):
    window_count, _, chan_rows, length = spectrum.shape
    first, second = factor_pair(length)
    shaped = spectrum.reshape(window_count, 2, chan_rows, first, second)
    section = product("wrcab,rask->wsckb", shaped, section_one(first, 1.0))
    result = product(
        "wsckb,skbj->wcjk", section, section_two(first, second, 1.0, scale)[:, :, :, 0, :]
    )
    return result.reshape(window_count, chan_rows, length)


def channel_transform(spectrum, direction, scale):
    window_count, _, length, columns = spectrum.shape
    first, second = factor_pair(length)
    shaped = spectrum.reshape(window_count, 2, first, second, columns)
    section = product("wrabm,rask->wskbm", shaped, section_one(first, direction))
    result = product("wskbm,skbtj->wtjkm", section, section_two(first, second, direction, scale))
    return result.reshape(window_count, 2, length, columns)


def per_device(tokens, head_weight, target, target_amp, patch_ranks):
    chan_count = lax.axis_size("chan")
    win_count = lax.axis_size("win")
    local_windows, local_patches, width = tokens.shape
    local_channels = target.shape[1]
    samples = target.shape[2]
    all_channels = local_channels * chan_count
    all_windows = local_windows * win_count
    channel_patches = local_channels // PATCH_C
    sample_patches = samples // PATCH_S
    pixels = PATCH_C * PATCH_S
    keep_count = local_patches * chan_count // 4
    column_count = samples // chan_count
    norm_scale = 1.0 / math.sqrt(all_channels * samples)
    patches = jnp.einsum(
        "wpe,ef->wpf", tokens, head_weight, preferred_element_type=jnp.float32
    ).astype(jnp.bfloat16)
    image = patches.reshape(local_windows, channel_patches, sample_patches, PATCH_C, PATCH_S)
    image = image.transpose(0, 1, 3, 2, 4).reshape(local_windows, local_channels, samples)
    masked = (patch_ranks >= keep_count).reshape(
        local_windows, channel_patches, 1, sample_patches, 1
    )
    pixel_mask = jnp.broadcast_to(
        masked, (local_windows, channel_patches, PATCH_C, sample_patches, PATCH_S)
    )
    pixel_mask = pixel_mask.reshape(local_windows, local_channels, samples)
    composite = jnp.where(pixel_mask, image, target)
    time_spectrum = time_forward(composite.astype(jnp.float32))
    amp_full = target_amp.astype(jnp.float32)
    spectrum = time_spectrum.reshape(local_windows, 2, local_channels, chan_count, column_count)
    amp_blocks = amp_full.reshape(local_windows, 1, local_channels, chan_count, column_count)
    spectrum_cols, amp_cols = (
        lax.all_to_all(spectrum, "chan", split_axis=3, concat_axis=2, tiled=True),
        lax.all_to_all(amp_blocks, "chan", split_axis=3, concat_axis=2, tiled=True),
    )
    freq = channel_transform(spectrum_cols[:, :, :, 0, :], -1.0, norm_scale)
    freq_real = freq[:, 0]
    freq_imag = freq[:, 1]
    amplitude = jnp.sqrt(freq_real * freq_real + freq_imag * freq_imag + 1.0)
    weighting = (amplitude - amp_cols[:, 0, :, 0, :]) / (amplitude * all_windows)
    back = channel_transform(freq * weighting[:, None], 1.0, 1.0)
    residual_cols = back[:, :, :, None, :]
    returned = lax.all_to_all(residual_cols, "chan", split_axis=2, concat_axis=3, tiled=True)
    returned = returned.reshape(local_windows, 2, local_channels, samples)
    image_real = time_inverse(returned, norm_scale)
    grad_image = jnp.where(pixel_mask, image_real, 0.0)
    grad_patches = grad_image.reshape(
        local_windows, channel_patches, PATCH_C, sample_patches, PATCH_S
    )
    grad_patches = (
        grad_patches.transpose(0, 1, 3, 2, 4)
        .reshape(local_windows, local_patches, pixels)
        .astype(jnp.bfloat16)
    )
    grad_tokens = jnp.einsum(
        "wpf,ef->wpe", grad_patches, head_weight, preferred_element_type=jnp.float32
    ).astype(jnp.bfloat16)
    own_rows = lax.psum_scatter(
        jnp.einsum("wpe,wpf->ef", tokens, grad_patches, preferred_element_type=jnp.float32),
        "chan",
        scatter_dimension=0,
        tiled=True,
    )
    grad_weight = lax.psum_scatter(own_rows, "win", scatter_dimension=1, tiled=True)
    return (grad_tokens, grad_weight)


def solution(mesh):
    in_specs = (
        P(("groups", "win"), "chan", None),
        P(),
        P(("groups", "win"), "chan", None),
        P(("groups", "win"), "chan", None),
        P(("groups", "win"), "chan"),
    )
    out_specs = (P(("groups", "win"), "chan", None), P(("groups", "chan"), "win"))
    return jax.shard_map(
        per_device, mesh=mesh, in_specs=in_specs, out_specs=out_specs, check_vma=False
    )
```

profile of v0, /device:TPU:0, one launch (start us, length us, event | category | flops | bytes accessed | tf_op | source)
XLA Modules:
  0.0 274.6 jit_solution(7919645180658135055)
XLA Ops:
  7.2 1.4 copy.107
  8.6 1.1 convert.2
  9.7 6.3 %all-to-all-start.1 = ((f32[1,1,128,4,512]{2,4,1,0,3:T(8,128)}), f32[1,1,128,4,512]{2,4,1,0,3:T(8,128)S(1)}, u32[]{:S(2)}, u32[]{:S(2)}) async-start(f32[1,1,128,4,512]{2,4,1,0,3:T(8,128)} %convert.2), calls=%async_computation.1 | async-start | bytes 2097152 | tf_op jit(solution)/shard_map/all_to_all | solution.py:112
  16.0 1.3 convolution_convert_fusion
  17.3 0.1 broadcast_in_dim.11
  17.4 0.2 broadcast_in_dim.13
  17.6 0.9 broadcast_in_dim.14
  18.5 1.8 reshape.543
  20.2 1.3 copy.191
  21.5 2.0 reshape.544
  23.6 1.2 select_n.210
  24.8 0.3 copy.97
  25.1 0.1 multiply_sine_fusion.4
  25.2 1.0 convolution_bitcast_fusion.1
  26.2 9.3 %multiply_sine_fusion.1 = (f32[32,64,1,64]{1,3,2,0:T(8,128)}, f32[32,64,1,64]{1,3,2,0:T(8,128)S(1)}, f32[32,64,1,64]{1,3,2,0:T(8,128)}, f32[32,64,1,64]{1,3,2,0:...) fusion(s32[64,64]{0,1:T(8,128)S(1)} %iota_multiply_fusion, s32[32,64]{1,0:T(8,128)S(1)} %iota_multiply_fusion.2), kind=kLoop, calls=%fused_computation.67 | loop fusion | flops 2228224 | bytes 3170304 | tf_op jit(solution)/shard_map/sin | solution.py:44
  35.5 0.6 maximum_bitcast_fusion.2
  36.1 5.1 %fusion.36 = f32[1,2,128,64,32]{2,3,1,4,0:T(8,128)S(1)} fusion(f32[2,128,32,64,1]{1,2,3,0,4:T(8,128)S(1)} %convolution_bitcast_fusion.1, f32[1,32,64,2,64]{2,4,0,3,1:T(8,128)S(1)} %get-tuple-element.15, f32[1,32,64,2,64]{2,4,0,3,1:T(8,128)S(1)} %get-tuple-element.14), kind=kOutput, calls=%fused_computation.37 | convolution fusion | flops 805830656 | bytes 6291456 | tf_op jit(solution)/shard_map/wsckb,skbtj->wtcjk/dot_general | solution.py:55
  41.2 1.2 copy.100
  42.5 1.5 copy.101
  43.9 1.0 copy-done.2
  44.9 5.1 %all-to-all-start = ((f32[1,2,128,4,512]{2,4,1,0,3:T(8,128)}), f32[1,2,128,4,512]{2,4,1,0,3:T(8,128)S(1)}, u32[]{:S(2)}, u32[]{:S(2)}) async-start(f32[1,2,128,4,512]{2,4,1,0,3:T(8,128)} %copy.101), calls=%async_computation | async-start | bytes 4194304 | tf_op jit(solution)/shard_map/all_to_all | solution.py:111
  50.0 0.1 fusion.89
  50.1 0.1 fusion.88
  50.1 0.1 multiply_sine_fusion.6
  50.2 0.1 multiply_sine_fusion.7
  50.3 2.0 multiply_sine_fusion.3
  52.3 1.1 maximum_bitcast_fusion.6
  53.4 1.1 maximum_bitcast_fusion.4
  54.5 2.6 copy.109
  57.1 40.5 %all-to-all-done = f32[1,2,128,4,512]{2,4,1,0,3:T(8,128)S(1)} async-done(((f32[1,2,128,4,512]{2,4,1,0,3:T(8,128)}), f32[1,2,128,4,512]{2,4,1,0,3:T(8,128)S(1)}, u32[]{:S(2)}, u32[]{:S(2)}) %all-to-all-start) | async-done | bytes 2097184 | tf_op jit(solution)/shard_map/all_to_all | solution.py:111
  97.6 2.0 copy.102
  99.6 4.6 %fusion.24 = f32[2,16,32,512,1]{3,1,2,0,4:T(8,128)S(1)} fusion(f32[2,16,32,512]{3,2,1,0:T(8,128)} %bitcast.180, f32[1,16,2,16]{1,3,0,2:T(8,128)S(1)} %get-tuple-element.37, f32[1,16,2,16]{1,3,0,2:T(8,128)S(1)} %get-tuple-element.36), kind=kOutput, calls=%fused_computation.33 | convolution fusion | flops 201327616 | bytes 4198400 | tf_op jit(solution)/shard_map/wrabm,rask->wskbm/dot_general | solution.py:74
  104.3 3.0 %fusion.27 = f32[1,2,32,16,512]{4,2,1,3,0:T(8,128)S(1)} fusion(f32[2,16,32,512,1]{3,1,2,0,4:T(8,128)S(1)} %fusion.24, f32[1,16,32,2,32]{2,4,0,3,1:T(8,128)S(1)} %copy-done.7, f32[1,16,32,2,32]{2,4,0,3,1:T(8,128)S(1)} %copy-done.6), kind=kOutput, calls=%fused_computation.34 | convolution fusion | flops 402784256 | bytes 4456448 | tf_op jit(solution)/shard_map/wskbm,skbtj->wtjkm/dot_general | solution.py:75
  107.3 1.2 copy.105
  108.6 0.5 fusion.59
  109.1 0.5 broadcast_multiply_fusion
  109.6 3.0 %fusion.30 = f32[2,16,32,512,1]{3,1,2,0,4:T(8,128)S(1)} fusion(f32[2,16,32,512]{3,2,1,0:T(8,128)S(1)} %broadcast_multiply_fusion, f32[1,16,2,16]{1,3,2,0:T(8,128)S(1)} %get-tuple-element.35, f32[1,16,2,16]{1,3,2,0:T(8,128)S(1)} %get-tuple-element.34), kind=kOutput, calls=%fused_computation.35 | convolution fusion | flops 201327616 | bytes 4198400 | tf_op jit(solution)/shard_map/wrabm,rask->wskbm/dot_general | solution.py:74
  112.6 3.3 %fusion.11 = f32[16,2,32,512,1]{3,2,1,0,4:T(8,128)S(1)} fusion(f32[2,16,32,512,1]{3,1,2,0,4:T(8,128)S(1)} %fusion.30, f32[1,16,32,2,32]{2,4,3,1,0:T(8,128)S(1)} %copy-done.5, f32[1,16,32,2,32]{2,4,3,1,0:T(8,128)S(1)} %copy-done.4), kind=kOutput, calls=%fused_computation.15 | convolution fusion | flops 402718720 | bytes 4456448 | tf_op jit(solution)/shard_map/wskbm,skbtj->wtjkm/dot_general | solution.py:75
  115.9 0.3 copy.190
  116.2 1.2 copy.114
  117.4 3.0 %copy.115 = f32[1,2,512,1,512]{4,1,3,0,2:T(2,128)} copy(f32[1,2,512,1,512]{4,2,1,3,0:T(8,128)S(1)} %bitcast.184) | data formatting | bytes 4194304 | tf_op jit(solution)/shard_map/broadcast_in_dim;reshape | solution.py:120
  120.4 4.5 %all-to-all-start.2 = ((f32[1,2,512,1,512]{4,1,3,0,2:T(2,128)}), f32[1,2,512,1,512]{4,1,3,0,2:T(2,128)}, u32[]{:S(2)}, u32[]{:S(2)}) async-start(f32[1,2,512,1,512]{4,1,3,0,2:T(2,128)} %copy.115), calls=%async_computation.2 | async-start | bytes 4194304 | tf_op jit(solution)/shard_map/all_to_all | solution.py:121
  124.8 0.0 reduce-scatter.3.cloned.1.call-start
  124.9 0.1 fusion.87
  125.0 0.1 multiply_sine_fusion.5
  125.1 4.3 %maximum_bitcast_fusion = (f32[1,32,64,2,64]{2,4,3,1,0:T(8,128)S(1)}, f32[1,32,64,2,64]{2,4,3,1,0:T(8,128)}) fusion(f32[32,64,1,64]{1,3,2,0:T(8,128)} %get-tuple-element.20, f32[32,64,1,64]{1,3,2,0:T(8,128)} %get-tuple-element.25, f32[32,64,1,64]{1,3,2,0:T(8,128)} %get-tuple-element.22), kind=kLoop, calls=%fused_computation.9 | loop fusion | flops 524288 | bytes 3670016 | tf_op jit(solution)/shard_map/stack | solution.py:47
  129.4 43.2 %all-to-all-done.2 = f32[1,2,512,1,512]{4,1,3,0,2:T(2,128)} async-done(((f32[1,2,512,1,512]{4,1,3,0,2:T(2,128)}), f32[1,2,512,1,512]{4,1,3,0,2:T(2,128)}, u32[]{:S(2)}, u32[]{:S(2)}) %all-to-all-start.2) | async-done | bytes 2097184 | tf_op jit(solution)/shard_map/all_to_all | solution.py:121
  172.6 3.4 %copy.116 = f32[1,2,512,1,512]{4,2,1,3,0:T(8,128)} copy(f32[1,2,512,1,512]{4,1,3,0,2:T(2,128)} %all-to-all-done.2) | data formatting | bytes 4194304 | tf_op jit(solution)/shard_map/all_to_all | solution.py:121
  175.9 3.1 %copy.117 = f32[1,2,128,4,1,512]{2,5,3,1,4,0:T(8,128)} copy(f32[1,2,128,4,1,512]{5,2,3,1,4,0:T(8,128)} %bitcast.185) | data formatting | bytes 4194304 | tf_op jit(solution)/shard_map/all_to_all | solution.py:121
  179.0 4.7 %fusion.33 = f32[2,128,32,64]{1,2,3,0:T(8,128)S(1)} fusion(f32[2,128,32,64]{1,3,2,0:T(8,128)} %bitcast.181, f32[1,32,2,32]{1,3,2,0:T(8,128)S(1)} %get-tuple-element.33, f32[1,32,2,32]{1,3,2,0:T(8,128)S(1)} %get-tuple-element.32), kind=kOutput, calls=%fused_computation.36 | convolution fusion | flops 402657280 | bytes 4210688 | tf_op jit(solution)/shard_map/wrcab,rask->wsckb/dot_general | solution.py:63
  183.8 4.3 %fusion.41 = bf16[1,128,64,32]{1,2,3,0:T(8,128)(2,1)} fusion(f32[2,128,32,64]{1,2,3,0:T(8,128)S(1)} %fusion.33, f32[1,32,64,2,64]{2,4,3,1,0:T(8,128)S(1)} %copy-done.1, f32[1,32,64,2,64]{2,4,3,1,0:T(8,128)S(1)} %get-tuple-element.12), kind=kOutput, calls=%fused_computation.42 | convolution fusion | flops 403177472 | bytes 4718592 | tf_op jit(solution)/shard_map/wsckb,skbj->wcjk/dot_general | solution.py:64
  188.1 4.5 %copy.121 = bf16[1,128,64,32]{3,2,1,0:T(8,128)(2,1)S(1)} copy(bf16[1,128,64,32]{1,2,3,0:T(8,128)(2,1)} %fusion.41) | data formatting | bytes 1048576 | tf_op jit(solution)/shard_map/wsckb,skbj->wcjk/transpose | solution.py:64
  192.6 1.8 reshape.554
  194.4 1.5 fusion.49
  195.9 0.4 copy.122
  196.3 0.7 convert_element_type.206
  197.1 1.8 convolution_bitcast_fusion
  198.9 0.0 reduce-scatter.3.cloned.1.call-update
  198.9 0.0 reduce-scatter.5.cloned.1.call-start
  198.9 43.1 %reduce-scatter.3.cloned.1.call-done = f32[128,1024]{0,1:T(8,128)} async-done(((f32[512,1024]{0,1:T(8,128)}), f32[128,1024]{0,1:T(8,128)}) %reduce-scatter.3.cloned.1.call-update) | async-done | bytes 524304 | tf_op jit(solution)/shard_map/reduce_scatter | solution.py:136
  242.0 0.0 reduce-scatter.5.cloned.1.call-update
  242.1 1.2 fusion.46
  243.2 22.4 %reduce-scatter.5.cloned.1.call-done = f32[128,256]{0,1:T(8,128)} async-done(((f32[128,1024]{0,1:T(8,128)}), f32[128,256]{0,1:T(8,128)}) %reduce-scatter.5.cloned.1.call-update) | async-done | bytes 131088 | tf_op jit(solution)/shard_map/reduce_scatter | solution.py:142
  265.7 1.7 copy.123
  (32 shorter events, 0.1 us)
Async XLA Ops:
  7.2 8.9 %copy-start = (bf16[512,1024]{1,0:T(8,128)(2,1)S(1)}, bf16[512,1024]{1,0:T(8,128)(2,1)}, u32[]{:S(2)}) copy-start(bf16[512,1024]{1,0:T(8,128)(2,1)} %param.6) | copy-start | bytes 3145732
  8.6 7.4 %copy-start.10 = (s32[1,256]{1,0:T(1,128)S(1)}, s32[1,256]{1,0:T(1,128)}, u32[]{:S(2)}) copy-start(s32[1,256]{1,0:T(1,128)} %param.9) | copy-start | bytes 3076
  8.6 7.4 %copy-start.8 = (bf16[1,256,512]{2,1,0:T(8,128)(2,1)S(1)}, bf16[1,256,512]{2,1,0:T(8,128)(2,1)}, u32[]{:S(2)}) copy-start(bf16[1,256,512]{2,1,0:T(8,128)(2,1)} %param.5) | copy-start | bytes 786436
  9.7 34.3 %all-to-all-start.1 = ((f32[1,1,128,4,512]{2,4,1,0,3:T(8,128)}), f32[1,1,128,4,512]{2,4,1,0,3:T(8,128)S(1)}, u32[]{:S(2)}, u32[]{:S(2)}) async-start(f32[1,1,128,4,512]{2,4,1,0,3:T(8,128)} %convert.2), calls=%async_computation.1 | async-start | bytes 2097152 | tf_op jit(solution)/shard_map/all_to_all | solution.py:112
  43.9 1.0 copy-start.2
  44.9 52.7 %all-to-all-start = ((f32[1,2,128,4,512]{2,4,1,0,3:T(8,128)}), f32[1,2,128,4,512]{2,4,1,0,3:T(8,128)S(1)}, u32[]{:S(2)}, u32[]{:S(2)}) async-start(f32[1,2,128,4,512]{2,4,1,0,3:T(8,128)} %copy.101), calls=%async_computation | async-start | bytes 4194304 | tf_op jit(solution)/shard_map/all_to_all | solution.py:111
  99.6 4.6 %copy-start.6 = (f32[1,16,32,2,32]{2,4,0,3,1:T(8,128)S(1)}, f32[1,16,32,2,32]{2,4,0,3,1:T(8,128)}, u32[]{:S(2)}) copy-start(f32[1,16,32,2,32]{2,4,0,3,1:T(8,128)} %get-tuple-element.18) | copy-start | bytes 393220
  99.6 4.6 %copy-start.7 = (f32[1,16,32,2,32]{2,4,0,3,1:T(8,128)S(1)}, f32[1,16,32,2,32]{2,4,0,3,1:T(8,128)}, u32[]{:S(2)}) copy-start(f32[1,16,32,2,32]{2,4,0,3,1:T(8,128)} %get-tuple-element.19) | copy-start | bytes 393220
  107.3 1.2 copy-start.3
  109.6 3.0 %copy-start.4 = (f32[1,16,32,2,32]{2,4,3,1,0:T(8,128)S(1)}, f32[1,16,32,2,32]{2,4,3,1,0:T(8,128)}, u32[]{:S(2)}) copy-start(f32[1,16,32,2,32]{2,4,3,1,0:T(8,128)} %get-tuple-element.16) | copy-start | bytes 393220
  109.6 3.0 %copy-start.5 = (f32[1,16,32,2,32]{2,4,3,1,0:T(8,128)S(1)}, f32[1,16,32,2,32]{2,4,3,1,0:T(8,128)}, u32[]{:S(2)}) copy-start(f32[1,16,32,2,32]{2,4,3,1,0:T(8,128)} %get-tuple-element.17) | copy-start | bytes 393220
  120.4 52.2 %all-to-all-start.2 = ((f32[1,2,512,1,512]{4,1,3,0,2:T(2,128)}), f32[1,2,512,1,512]{4,1,3,0,2:T(2,128)}, u32[]{:S(2)}, u32[]{:S(2)}) async-start(f32[1,2,512,1,512]{4,1,3,0,2:T(2,128)} %copy.115), calls=%async_computation.2 | async-start | bytes 4194304 | tf_op jit(solution)/shard_map/all_to_all | solution.py:121
  124.8 117.2 %reduce-scatter.3.cloned.1.call-start = ((), (), s32[]{:S(2)}) async-start(), calls=%async_computation.5 | async-start | bytes 2621440 | tf_op jit(solution)/shard_map/reduce_scatter | solution.py:136
  179.0 4.8 %copy-start.1 = (f32[1,32,64,2,64]{2,4,3,1,0:T(8,128)S(1)}, f32[1,32,64,2,64]{2,4,3,1,0:T(8,128)}, u32[]{:S(2)}) copy-start(f32[1,32,64,2,64]{2,4,3,1,0:T(8,128)} %get-tuple-element.13) | copy-start | bytes 3145732
  195.9 1.2 copy-start.9
  198.9 66.8 %reduce-scatter.5.cloned.1.call-start = ((), (), s32[]{:S(2)}) async-start(), calls=%async_computation.6 | async-start | bytes 655360 | tf_op jit(solution)/shard_map/reduce_scatter | solution.py:142
Sparse Core Ops, SparseCore 0:
  199.0 42.9 reduce-scatter.2
  244.7 20.9 reduce-scatter.4
where the time goes:
time: 280 us; the launch traced here: 275 us
  waiting for transfers between devices  149 us (53%)
  local copies, waits for them, and re-layouts  37.3 us (13%)
  matrix products  33.3 us (12%)
  other arithmetic  23.8 us (8%)
  starting transfers between devices  15.9 us (6%)
  between operations  14.9 us (5%)
    all_to_all x1, waiting for transfers between devices, per_device(): lax.all_to_all(residual_cols, 'chan', split_axis=2, concat_axis=3, tiled=...  43.2 us
    reduce_scatter x1, waiting for transfers between devices, per_device(): lax.psum_scatter(jnp.einsum('wpe,wpf->ef', tokens, grad_patches, preferre...  43.1 us
    all_to_all x1, waiting for transfers between devices, per_device(): lax.all_to_all(spectrum, 'chan', split_axis=3, concat_axis=2, tiled=True)  40.5 us
    reduce_scatter x1, waiting for transfers between devices, per_device(): lax.psum_scatter(own_rows, 'win', scatter_dimension=1, tiled=True)  22.4 us
    sin x2, other arithmetic, section_two(): sine = jnp.sin(angles)  11.2 us
    dot_general x2, matrix products, channel_transform(): product('wrabm,rask->wskbm', shaped, section_one(first, direction))  7.62 us
    another operation x4, other arithmetic, section_two(): return jnp.stack([upper, lower], axis=0) * scale  7.17 us
    all_to_all x2, local copies, waits for them, and re-layouts, per_device(): lax.all_to_all(residual_cols, 'chan', split_axis=2, concat_axis=3, tiled=...  6.44 us
  transfers between devices with their start and end apart: 5, of which 4 were waited for; matrix products, arithmetic and copies ran while one was open for 15% of the time, Pallas kernels for 0%

commit v1 on v0

--- a/solution.py
+++ b/solution.py
@@ -107,9 +107,29 @@
     amp_full = target_amp.astype(jnp.float32)
     spectrum = time_spectrum.reshape(local_windows, 2, local_channels, chan_count, column_count)
     amp_blocks = amp_full.reshape(local_windows, 1, local_channels, chan_count, column_count)
+
+    def launch_masks(panel):
+        named_axis = "chan"
+        carry_in, res = (lax.axis_size(named_axis), lax.axis_index(named_axis))
+        w_next = list(panel.shape)
+        local_next = panel.shape[3] // carry_in
+        w_next[3] = local_next
+        top = w_next[2]
+        w_next[2] = top * carry_in
+        now = jnp.zeros(w_next, panel.dtype)
+        for at in range(carry_in):
+            y = lax.dynamic_slice_in_dim(panel, (res ^ at) * local_next, local_next, axis=3)
+            if at:
+                ledger = []
+                for s in range(carry_in):
+                    ledger.append((s, s ^ at))
+                y = lax.ppermute(y, named_axis, perm=ledger)
+            now = lax.dynamic_update_slice_in_dim(now, y, (res ^ at) * top, axis=2)
+        return now
+
     spectrum_cols, amp_cols = (
         lax.all_to_all(spectrum, "chan", split_axis=3, concat_axis=2, tiled=True),
-        lax.all_to_all(amp_blocks, "chan", split_axis=3, concat_axis=2, tiled=True),
+        launch_masks(amp_blocks),
     )
     freq = channel_transform(spectrum_cols[:, :, :, 0, :], -1.0, norm_scale)
     freq_real = freq[:, 0]

time: 280 us -> 293 us (1.046)
  local copies, waits for them, and re-layouts: 37.3 us -> 46.1 us
  other arithmetic: 23.8 us -> 26.9 us
  waiting for transfers between devices: 149 us -> 152 us
    ppermute x0 -> x3, waiting for transfers between devices: none -> 41.3 us  [launch_masks(): y = lax.ppermute(y, named_axis, perm=ledger)]
    all_to_all x1, waiting for transfers between devices: 40.5 us -> 0.01 us  [per_device(): lax.all_to_all(spectrum, 'chan', split_axis=3, concat_axis=2, tiled=True)]
    all_to_all x1 -> x0, starting transfers between devices: 6.32 us -> none  [per_device(): lax.all_to_all(amp_blocks, 'chan', split_axis=3, concat_axis=2, tiled=True)]
    dynamic_update_slice x0 -> x4, local copies, waits for them, and re-layouts: none -> 5.73 us  [launch_masks(): now = lax.dynamic_update_slice_in_dim(now, y, (res ^ at) * top, axis=2)]
    unnamed x24 -> x21, local copies, waits for them, and re-layouts: 4.07 us -> 9.11 us
    ppermute x0 -> x3, starting transfers between devices: none -> 4.39 us  [launch_masks(): y = lax.ppermute(y, named_axis, perm=ledger)]
  transfers between devices with their start and end apart: 5 -> 7, of which waited for: 4 -> 5; matrix products, arithmetic and copies ran while one was open for 15% -> 10% of each run, Pallas kernels for 0% -> 0%
where the time goes in v1:
time: 293 us; the launch traced here: 288 us
  waiting for transfers between devices  152 us (52%)
  local copies, waits for them, and re-layouts  46.1 us (16%)
  matrix products  33.4 us (11%)
  other arithmetic  26.9 us (9%)
  starting transfers between devices  15.7 us (5%)
  between operations  14.9 us (5%)
    reduce_scatter x1, waiting for transfers between devices, per_device(): lax.psum_scatter(jnp.einsum('wpe,wpf->ef', tokens, grad_patches, preferre...  44.4 us
    all_to_all x1, waiting for transfers between devices, per_device(): lax.all_to_all(residual_cols, 'chan', split_axis=2, concat_axis=3, tiled=...  43.4 us
    ppermute x3, waiting for transfers between devices, launch_masks(): y = lax.ppermute(y, named_axis, perm=ledger)  41.3 us
    reduce_scatter x1, waiting for transfers between devices, per_device(): lax.psum_scatter(own_rows, 'win', scatter_dimension=1, tiled=True)  22.4 us
    sin x2, other arithmetic, section_two(): sine = jnp.sin(angles)  11.3 us
    unnamed x21, local copies, waits for them, and re-layouts  9.11 us
    dot_general x2, matrix products, channel_transform(): product('wrabm,rask->wskbm', shaped, section_one(first, direction))  7.62 us
    another operation x4, other arithmetic, section_two(): return jnp.stack([upper, lower], axis=0) * scale  7.16 us
  transfers between devices with their start and end apart: 7, of which 5 were waited for; matrix products, arithmetic and copies ran while one was open for 10% of the time, Pallas kernels for 0%

profile of v1, /device:TPU:0, one launch (start us, length us, event | category | flops | bytes accessed | tf_op | source)
XLA Modules:
  0.0 288.5 jit_solution(6791045913425150805)
XLA Ops:
  7.3 0.8 compare_reduce_fusion
  8.1 0.1 broadcast_in_dim.11
  8.2 0.2 broadcast_in_dim.13
  8.4 0.9 broadcast_in_dim.14
  9.3 1.4 convolution_convert_fusion
  10.7 0.7 reshape.590
  11.3 0.3 copy.201
  11.6 0.8 reshape.591
  12.4 1.2 select_n.234
  13.7 0.3 copy.102
  13.9 9.4 %multiply_sine_fusion.1 = (f32[32,64,1,64]{1,3,2,0:T(8,128)}, f32[32,64,1,64]{1,3,2,0:T(8,128)S(1)}, f32[32,64,1,64]{1,3,2,0:T(8,128)}, f32[32,64,1,64]{1,3,2,0:...) fusion(s32[64,64]{0,1:T(8,128)S(1)} %iota_multiply_fusion, s32[32,64]{1,0:T(8,128)S(1)} %iota_multiply_fusion.2), kind=kLoop, calls=%fused_computation.67 | loop fusion | flops 2228224 | bytes 3170304 | tf_op jit(solution)/shard_map/sin | solution.py:44
  23.3 0.6 maximum_bitcast_fusion.2
  23.9 1.0 convolution_bitcast_fusion.1
  24.9 5.1 %fusion.36 = f32[1,2,128,64,32]{2,3,1,4,0:T(8,128)S(1)} fusion(f32[2,128,32,64,1]{1,2,3,0,4:T(8,128)S(1)} %convolution_bitcast_fusion.1, f32[1,32,64,2,64]{2,4,0,3,1:T(8,128)S(1)} %get-tuple-element.19, f32[1,32,64,2,64]{2,4,0,3,1:T(8,128)S(1)} %get-tuple-element.18), kind=kOutput, calls=%fused_computation.37 | convolution fusion | flops 805830656 | bytes 6291456 | tf_op jit(solution)/shard_map/wsckb,skbtj->wtcjk/dot_general | solution.py:55
  30.0 1.2 copy.105
  31.3 1.5 copy.106
  32.7 6.5 %all-to-all-start = ((f32[1,2,128,4,512]{2,4,1,0,3:T(8,128)}), f32[1,2,128,4,512]{2,4,1,0,3:T(8,128)S(1)}, u32[]{:S(2)}, u32[]{:S(2)}) async-start(f32[1,2,128,4,512]{2,4,1,0,3:T(8,128)} %copy.106), calls=%async_computation | async-start | bytes 4194304 | tf_op jit(solution)/shard_map/all_to_all | solution.py:131
  39.2 2.0 copy.112
  41.3 2.1 convert.1
  43.4 2.1 constant_dynamic-slice_fusion
  45.5 1.8 copy.155
  47.2 2.0 collective-permute-start
  49.3 1.8 copy.156
  51.0 2.4 collective-permute-start.1
  53.4 1.8 copy.157
  55.2 0.8 copy.113
  56.3 2.0 multiply_sine_fusion.3
  58.3 1.1 maximum_bitcast_fusion.6
  59.4 1.1 squeeze.17
  60.5 0.7 bitcast_dynamic-update-slice_fusion.3
  61.3 1.2 maximum_bitcast_fusion.4
  62.4 17.6 %collective-permute-done = f32[1,1,128,1,512]{4,2,3,1,0:T(8,128)} collective-permute-done((f32[1,1,128,1,512]{4,2,3,1,0:T(8,128)}, f32[1,1,128,1,512]{4,2,3,1,0:T(8,128)}, u32[]{:S(2)}, u32[]{:S(2)}) %collective-permute-start) | collective-permute-done | bytes 262176 | tf_op jit(solution)/shard_map/ppermute | solution.py:126
  80.0 1.7 bitcast_dynamic-update-slice_fusion.2
  81.6 23.8 %collective-permute-done.1 = f32[1,1,128,1,512]{4,2,3,1,0:T(8,128)} collective-permute-done((f32[1,1,128,1,512]{4,2,3,1,0:T(8,128)}, f32[1,1,128,1,512]{4,2,3,1,0:T(8,128)}, u32[]{:S(2)}, u32[]{:S(2)}) %collective-permute-start.1) | collective-permute-done | bytes 262176 | tf_op jit(solution)/shard_map/ppermute | solution.py:126
  105.4 1.7 bitcast_dynamic-update-slice_fusion.1
  107.1 1.7 bitcast_dynamic-update-slice_fusion
  108.7 1.8 copy.107
  110.6 4.6 %fusion.24 = f32[2,16,32,512,1]{3,1,2,0,4:T(8,128)S(1)} fusion(f32[2,16,32,512]{3,2,1,0:T(8,128)} %bitcast.181, f32[1,16,2,16]{1,3,0,2:T(8,128)S(1)} %get-tuple-element.41, f32[1,16,2,16]{1,3,0,2:T(8,128)S(1)} %get-tuple-element.40), kind=kOutput, calls=%fused_computation.33 | convolution fusion | flops 201327616 | bytes 4198400 | tf_op jit(solution)/shard_map/wrabm,rask->wskbm/dot_general | solution.py:74
  115.2 3.0 %fusion.27 = f32[1,2,32,16,512]{4,2,1,3,0:T(8,128)S(1)} fusion(f32[2,16,32,512,1]{3,1,2,0,4:T(8,128)S(1)} %fusion.24, f32[1,16,32,2,32]{2,4,0,3,1:T(8,128)S(1)} %copy-done.5, f32[1,16,32,2,32]{2,4,0,3,1:T(8,128)S(1)} %copy-done.4), kind=kOutput, calls=%fused_computation.34 | convolution fusion | flops 402784256 | bytes 4456448 | tf_op jit(solution)/shard_map/wskbm,skbtj->wtjkm/dot_general | solution.py:75
  118.3 1.2 copy.110
  119.5 1.7 multiply_divide_fusion
  121.2 0.5 broadcast_multiply_fusion
  121.7 3.0 %fusion.30 = f32[2,16,32,512,1]{3,1,2,0,4:T(8,128)S(1)} fusion(f32[2,16,32,512]{3,2,1,0:T(8,128)S(1)} %broadcast_multiply_fusion, f32[1,16,2,16]{1,3,2,0:T(8,128)S(1)} %get-tuple-element.39, f32[1,16,2,16]{1,3,2,0:T(8,128)S(1)} %get-tuple-element.38), kind=kOutput, calls=%fused_computation.35 | convolution fusion | flops 201327616 | bytes 4198400 | tf_op jit(solution)/shard_map/wrabm,rask->wskbm/dot_general | solution.py:74
  124.8 3.3 %fusion.11 = f32[16,2,32,512,1]{3,2,1,0,4:T(8,128)S(1)} fusion(f32[2,16,32,512,1]{3,1,2,0,4:T(8,128)S(1)} %fusion.30, f32[1,16,32,2,32]{2,4,3,1,0:T(8,128)S(1)} %copy-done.3, f32[1,16,32,2,32]{2,4,3,1,0:T(8,128)S(1)} %copy-done.2), kind=kOutput, calls=%fused_computation.15 | convolution fusion | flops 402718720 | bytes 4456448 | tf_op jit(solution)/shard_map/wskbm,skbtj->wtjkm/dot_general | solution.py:75
  128.1 0.3 copy.200
  128.3 1.2 copy.121
  129.6 3.0 %copy.122 = f32[1,2,512,1,512]{4,1,3,0,2:T(2,128)} copy(f32[1,2,512,1,512]{4,2,1,3,0:T(8,128)S(1)} %bitcast.185) | data formatting | bytes 4194304 | tf_op jit(solution)/shard_map/broadcast_in_dim;reshape | solution.py:140
  132.5 4.7 %all-to-all-start.1 = ((f32[1,2,512,1,512]{4,1,3,0,2:T(2,128)}), f32[1,2,512,1,512]{4,1,3,0,2:T(2,128)}, u32[]{:S(2)}, u32[]{:S(2)}) async-start(f32[1,2,512,1,512]{4,1,3,0,2:T(2,128)} %copy.122), calls=%async_computation.1 | async-start | bytes 4194304 | tf_op jit(solution)/shard_map/all_to_all | solution.py:141
  137.5 4.3 %maximum_bitcast_fusion = (f32[1,32,64,2,64]{2,4,3,1,0:T(8,128)S(1)}, f32[1,32,64,2,64]{2,4,3,1,0:T(8,128)}) fusion(f32[32,64,1,64]{1,3,2,0:T(8,128)} %get-tuple-element.24, f32[32,64,1,64]{1,3,2,0:T(8,128)} %get-tuple-element.29, f32[32,64,1,64]{1,3,2,0:T(8,128)} %get-tuple-element.26), kind=kLoop, calls=%fused_computation.9 | loop fusion | flops 524288 | bytes 3670016 | tf_op jit(solution)/shard_map/stack | solution.py:47
  141.8 43.4 %all-to-all-done.1 = f32[1,2,512,1,512]{4,1,3,0,2:T(2,128)} async-done(((f32[1,2,512,1,512]{4,1,3,0,2:T(2,128)}), f32[1,2,512,1,512]{4,1,3,0,2:T(2,128)}, u32[]{:S(2)}, u32[]{:S(2)}) %all-to-all-start.1) | async-done | bytes 2097184 | tf_op jit(solution)/shard_map/all_to_all | solution.py:141
  185.2 3.4 %copy.123 = f32[1,2,512,1,512]{4,2,1,3,0:T(8,128)} copy(f32[1,2,512,1,512]{4,1,3,0,2:T(2,128)} %all-to-all-done.1) | data formatting | bytes 4194304 | tf_op jit(solution)/shard_map/all_to_all | solution.py:141
  188.5 3.1 %copy.124 = f32[1,2,128,4,1,512]{2,5,3,1,4,0:T(8,128)} copy(f32[1,2,128,4,1,512]{5,2,3,1,4,0:T(8,128)} %bitcast.186) | data formatting | bytes 4194304 | tf_op jit(solution)/shard_map/all_to_all | solution.py:141
  191.6 4.7 %fusion.33 = f32[2,128,32,64]{1,2,3,0:T(8,128)S(1)} fusion(f32[2,128,32,64]{1,3,2,0:T(8,128)} %bitcast.182, f32[1,32,2,32]{1,3,2,0:T(8,128)S(1)} %get-tuple-element.37, f32[1,32,2,32]{1,3,2,0:T(8,128)S(1)} %get-tuple-element.36), kind=kOutput, calls=%fused_computation.36 | convolution fusion | flops 402657280 | bytes 4210688 | tf_op jit(solution)/shard_map/wrcab,rask->wsckb/dot_general | solution.py:63
  196.4 4.3 %fusion.41 = bf16[1,128,64,32]{1,2,3,0:T(8,128)(2,1)} fusion(f32[2,128,32,64]{1,2,3,0:T(8,128)S(1)} %fusion.33, f32[1,32,64,2,64]{2,4,3,1,0:T(8,128)S(1)} %copy-done.1, f32[1,32,64,2,64]{2,4,3,1,0:T(8,128)S(1)} %get-tuple-element.12), kind=kOutput, calls=%fused_computation.42 | convolution fusion | flops 403177472 | bytes 4718592 | tf_op jit(solution)/shard_map/wsckb,skbj->wcjk/dot_general | solution.py:64
  200.6 4.5 %copy.128 = bf16[1,128,64,32]{3,2,1,0:T(8,128)(2,1)S(1)} copy(bf16[1,128,64,32]{1,2,3,0:T(8,128)(2,1)} %fusion.41) | data formatting | bytes 1048576 | tf_op jit(solution)/shard_map/wsckb,skbj->wcjk/transpose | solution.py:64
  205.2 1.8 reshape.601
  207.0 1.5 fusion.49
  208.5 0.4 copy.129
  208.9 0.7 convert_element_type.206
  209.6 1.8 convolution_bitcast_fusion
  211.5 44.4 %reduce-scatter.3.cloned.1.call-done = f32[128,1024]{0,1:T(8,128)} async-done(((f32[512,1024]{0,1:T(8,128)}), f32[128,1024]{0,1:T(8,128)}) %reduce-scatter.3.cloned.1.call-update) | async-done | bytes 524304 | tf_op jit(solution)/shard_map/reduce_scatter | solution.py:156
  255.9 1.2 fusion.46
  257.1 22.4 %reduce-scatter.5.cloned.1.call-done = f32[128,256]{0,1:T(8,128)} async-done(((f32[128,1024]{0,1:T(8,128)}), f32[128,256]{0,1:T(8,128)}) %reduce-scatter.5.cloned.1.call-update) | async-done | bytes 131088 | tf_op jit(solution)/shard_map/reduce_scatter | solution.py:162
  279.5 1.7 copy.130
  (39 shorter events, 0.7 us)
Async XLA Ops:
  7.2 2.1 copy-start
  32.7 76.0 %all-to-all-start = ((f32[1,2,128,4,512]{2,4,1,0,3:T(8,128)}), f32[1,2,128,4,512]{2,4,1,0,3:T(8,128)S(1)}, u32[]{:S(2)}, u32[]{:S(2)}) async-start(f32[1,2,128,4,512]{2,4,1,0,3:T(8,128)} %copy.106), calls=%async_computation | async-start | bytes 4194304 | tf_op jit(solution)/shard_map/all_to_all | solution.py:131
  47.2 32.7 %collective-permute-start = (f32[1,1,128,1,512]{4,2,3,1,0:T(8,128)}, f32[1,1,128,1,512]{4,2,3,1,0:T(8,128)}, u32[]{:S(2)}, u32[]{:S(2)}) collective-permute-start(f32[1,1,128,1,512]{4,2,3,1,0:T(8,128)} %copy.155), channel_id=1, source_target_pairs={{0,4},{4,0},{8,12},{12,8},{1,5},{5,1},{9,13},{13,9},{2,6},{6,2},{1... | collective-permute-start | bytes 786440 | tf_op jit(solution)/shard_map/ppermute | solution.py:126
  51.0 54.4 %collective-permute-start.1 = (f32[1,1,128,1,512]{4,2,3,1,0:T(8,128)}, f32[1,1,128,1,512]{4,2,3,1,0:T(8,128)}, u32[]{:S(2)}, u32[]{:S(2)}) collective-permute-start(f32[1,1,128,1,512]{4,2,3,1,0:T(8,128)} %copy.156), channel_id=1, source_target_pairs={{0,8},{4,12},{8,0},{12,4},{1,9},{5,13},{9,1},{13,5},{2,10},{6,14},... | collective-permute-start | bytes 786440 | tf_op jit(solution)/shard_map/ppermute | solution.py:126
  55.2 51.9 %collective-permute-start.2 = (f32[1,1,128,1,512]{4,2,3,1,0:T(8,128)}, f32[1,1,128,1,512]{4,2,3,1,0:T(8,128)}, u32[]{:S(2)}, u32[]{:S(2)}) collective-permute-start(f32[1,1,128,1,512]{4,2,3,1,0:T(8,128)} %copy.157), channel_id=1, source_target_pairs={{0,12},{4,8},{8,4},{12,0},{1,13},{5,9},{9,5},{13,1},{2,14},{6,10},... | collective-permute-start | bytes 786440 | tf_op jit(solution)/shard_map/ppermute | solution.py:126
  56.3 4.2 %copy-start.6 = (f32[1,1,128,1,512]{4,2,3,1,0:T(8,128)S(1)}, f32[1,1,128,1,512]{4,2,3,1,0:T(8,128)}, u32[]{:S(2)}) copy-start(f32[1,1,128,1,512]{4,2,3,1,0:T(8,128)} %copy.113) | copy-start | bytes 786436
  110.6 4.6 %copy-start.4 = (f32[1,16,32,2,32]{2,4,0,3,1:T(8,128)S(1)}, f32[1,16,32,2,32]{2,4,0,3,1:T(8,128)}, u32[]{:S(2)}) copy-start(f32[1,16,32,2,32]{2,4,0,3,1:T(8,128)} %get-tuple-element.22) | copy-start | bytes 393220
  110.6 4.6 %copy-start.5 = (f32[1,16,32,2,32]{2,4,0,3,1:T(8,128)S(1)}, f32[1,16,32,2,32]{2,4,0,3,1:T(8,128)}, u32[]{:S(2)}) copy-start(f32[1,16,32,2,32]{2,4,0,3,1:T(8,128)} %get-tuple-element.23) | copy-start | bytes 393220
  121.7 3.0 %copy-start.2 = (f32[1,16,32,2,32]{2,4,3,1,0:T(8,128)S(1)}, f32[1,16,32,2,32]{2,4,3,1,0:T(8,128)}, u32[]{:S(2)}) copy-start(f32[1,16,32,2,32]{2,4,3,1,0:T(8,128)} %get-tuple-element.20) | copy-start | bytes 393220
  121.7 3.0 %copy-start.3 = (f32[1,16,32,2,32]{2,4,3,1,0:T(8,128)S(1)}, f32[1,16,32,2,32]{2,4,3,1,0:T(8,128)}, u32[]{:S(2)}) copy-start(f32[1,16,32,2,32]{2,4,3,1,0:T(8,128)} %get-tuple-element.21) | copy-start | bytes 393220
  132.5 52.6 %all-to-all-start.1 = ((f32[1,2,512,1,512]{4,1,3,0,2:T(2,128)}), f32[1,2,512,1,512]{4,1,3,0,2:T(2,128)}, u32[]{:S(2)}, u32[]{:S(2)}) async-start(f32[1,2,512,1,512]{4,1,3,0,2:T(2,128)} %copy.122), calls=%async_computation.1 | async-start | bytes 4194304 | tf_op jit(solution)/shard_map/all_to_all | solution.py:141
  137.3 118.6 %reduce-scatter.3.cloned.1.call-start = ((), (), s32[]{:S(2)}) async-start(), calls=%async_computation.4 | async-start | bytes 2621440 | tf_op jit(solution)/shard_map/reduce_scatter | solution.py:156
  191.6 4.7 %copy-start.1 = (f32[1,32,64,2,64]{2,4,3,1,0:T(8,128)S(1)}, f32[1,32,64,2,64]{2,4,3,1,0:T(8,128)}, u32[]{:S(2)}) copy-start(f32[1,32,64,2,64]{2,4,3,1,0:T(8,128)} %get-tuple-element.13) | copy-start | bytes 3145732
  208.5 1.2 copy-start.7
  211.4 68.1 %reduce-scatter.5.cloned.1.call-start = ((), (), s32[]{:S(2)}) async-start(), calls=%async_computation.5 | async-start | bytes 655360 | tf_op jit(solution)/shard_map/reduce_scatter | solution.py:162
Sparse Core Ops, SparseCore 0:
  211.6 44.2 reduce-scatter.2
  258.5 20.9 reduce-scatter.4
